TPU v7x, 32 devices: a whole 2x2x4 slice. The times are simulated.
32 devices in a mesh: dp: 2 (over y), latent: 16 (over z, x, core).
Axes of the slice: x: 2, y: 2, z: 4, core: 2. Of those that a mesh axis runs over, the one named last changes fastest.
Arguments:
- resid: bfloat16 [128, 4608], P('dp'), may hold values from -24 to 24
- enc_weight: bfloat16 [4608, 131072], P(None, ('dp', 'latent')), may hold values from -0.09375 to 0.09375
- enc_bias: float32 [131072], P(('dp', 'latent')), may hold values from -3 to 3
- thresholds: float32 [131072], P(('dp', 'latent')), may hold values from 0.5 to 3
- dec_weight: bfloat16 [131072, 4608], P(('dp', 'latent')), may hold values from -0.09375 to 0.09375
- dec_bias: float32 [4608], replicated, may hold values from -7 to 7
- refusal_ids: int32 [16], replicated, may hold values from 0 to 131071, as said below
- clamp_levels: int32 [16], replicated, may hold values from 1 to 8
Outputs:
- steered: bfloat16 [128, 4608], P('dp')
Inputs may be any that keep to these rules, and one draw needn't show every extreme that they name: `refusal_ids`: an index may be named more than once, with different clamp levels.
All inputs are finite; a program needn't handle non-finite values.
Results may differ from a plain program's by a relative error of at most 0.0052.
Values may be sent and summed in bfloat16 or wider, within the bound.
A program may use at most 128 MiB of HBM per device.

v0:
```python
import jax
import jax.numpy as jnp
from jax import lax
from jax.sharding import PartitionSpec as P

gate_width = 0.1
norm_eps = 1e-06


def gate_latents(pre_acts, thresh_part):
    return pre_acts * jax.nn.sigmoid((pre_acts - thresh_part) / gate_width)


def clamp_block(activations, columns, refusal_ids, clamp_levels, thresh_part):
    matched = refusal_ids[:, None] == columns[None, :]
    targets_all = clamp_levels.astype(jnp.float32)[:, None] * thresh_part[None, :]
    targets = jnp.max(jnp.where(matched, targets_all, -1.0), axis=0)
    is_named = jnp.any(matched, axis=0)
    return jnp.where(is_named[None, :], jnp.maximum(activations, targets[None, :]), activations)


def body(resid, enc_weight, enc_bias, thresholds, dec_weight, dec_bias, refusal_ids, clamp_levels):
    lat_dev = enc_weight.shape[1]
    tok_dev = resid.shape[0]
    lat_count = lax.axis_size("latent")
    lat_index = lax.axis_index("latent")
    first_col = (lax.axis_index("dp") * lat_count + lat_index) * lat_dev
    columns = first_col + jnp.arange(lat_dev, dtype=jnp.int32)
    pre_acts = (
        jnp.dot(
            lax.all_gather(resid, "dp", axis=0, tiled=True),
            enc_weight,
            preferred_element_type=jnp.float32,
        )
        + enc_bias
    )
    activations = gate_latents(pre_acts, thresholds)
    clamped = clamp_block(activations, columns, refusal_ids, clamp_levels, thresholds).astype(
        jnp.bfloat16
    )
    rows_out = tok_dev // lat_count
    row_share = (
        lax.psum_scatter(
            jnp.dot(clamped, dec_weight, preferred_element_type=jnp.float32),
            ("dp", "latent"),
            scatter_dimension=0,
            tiled=True,
        )
        + dec_bias
    )
    own_rows = lax.dynamic_slice_in_dim(resid, lat_index * rows_out, rows_out, 0)
    in_sq = jnp.sum(jnp.square(own_rows.astype(jnp.float32)), axis=1, keepdims=True)
    out_sq = jnp.sum(jnp.square(row_share), axis=1, keepdims=True)
    scaled = (row_share * jnp.sqrt((in_sq + norm_eps) / (out_sq + norm_eps))).astype(jnp.bfloat16)
    steered = lax.all_gather(scaled, "latent", axis=0, tiled=True)
    return steered


def solution(mesh):
    in_specs = (
        P("dp", None),
        P(None, ("dp", "latent")),
        P(("dp", "latent")),
        P(("dp", "latent")),
        P(("dp", "latent"), None),
        P(),
        P(),
        P(),
    )
    out_specs = P("dp", None)
    return jax.shard_map(body, mesh=mesh, in_specs=in_specs, out_specs=out_specs, check_vma=False)
```

profile of v0, /device:TPU:0, one launch (start us, length us, event | category | flops | bytes accessed | tf_op | source)
XLA Modules:
  0.0 229.0 jit_solution(15462244859620577587)
XLA Ops:
  6.5 0.0 all-gather.3.cloned.1.call-start
  6.5 0.7 all-gather.3.cloned.1.call-update
  7.3 0.0 all-reduce.3.cloned.1.call-start
  7.3 0.7 convert_element_type.12
  8.0 0.8 compare_reduce_fusion
  8.8 0.9 fusion.8
  9.6 24.8 %all-gather.3.cloned.1.call-done = bf16[128,4608]{1,0:T(8,128)(2,1)} async-done(((bf16[64,4608]{1,0:T(8,128)(2,1)}), bf16[128,4608]{1,0:T(8,128)(2,1)}) %all-gather.3.cloned.1.call-update) | async-done | bytes 1179664 | tf_op jit(solution)/shard_map/all_gather | solution.py:31
  34.4 27.5 %fusion.1 = f32[128,4608]{1,0:T(8,128)} fusion(bf16[4096,4608]{1,0:T(8,128)(2,1)} %param.12, bf16[128,4608]{1,0:T(8,128)(2,1)} %all-gather.3.cloned.1.call-done, bf16[4608,4096]{1,0:T(8,128)(2,1)} %param.9, bf16[4096]{0:T(1024)(128)(2,1)S(1)} %fusion.8, f32[4096]{0:T(1024)} %param.11, f32[4096]{0:T(1024)} %param.10, pred[4096]{0:T(1024)(128)(4,1)S(1)} %compare_reduce_fusion), kind=kOutput, calls=%fused_computation.3 | convolution fusion | flops 9669443584 | bytes 79081472 | tf_op jit(solution)/shard_map/dot_general | solution.py:44
  61.9 0.0 copy-start
  61.9 0.0 all-reduce.3.cloned.1.call-update
  62.0 1.0 multiply_reduce_fusion.1
  63.0 134.3 %all-reduce.3.cloned.1.call-done = f32[128,4608]{1,0:T(8,128)} async-done(((f32[128,4608]{1,0:T(8,128)}), f32[128,4608]{1,0:T(8,128)}) %all-reduce.3.cloned.1.call-update) | async-done | bytes 2359312
  197.3 0.0 copy-done
  197.3 1.1 multiply_reduce_fusion
  198.3 1.0 fusion.9
  199.3 21.9 %all-gather = bf16[16,4,4608]{2,1,0:T(4,128)(2,1)S(1)} all-gather(bf16[1,4,4608]{2,1,0:T(4,128)(2,1)S(1)} %fusion.9), channel_id=1, replica_groups=mesh['dp'=2,'latent'=16] {'latent'}, dimensions={0}, use_global_device_ids=true | all-gather | bytes 626688 | tf_op jit(solution)/shard_map/all_gather | solution.py:55
  221.3 0.9 reshape.24
  (2 shorter events, 0.0 us)
Async XLA Ops:
  6.5 27.9 %all-gather.3.cloned.1.call-start = ((), (), s32[]{:S(2)}) async-start(), calls=%async_computation | async-start | bytes 1769472 | tf_op jit(solution)/shard_map/all_gather | solution.py:31
  7.3 190.0 %all-reduce.3.cloned.1.call-start = ((), (), s32[]{:S(2)}) async-start(), calls=%async_computation.1 | async-start | bytes 4718592
  61.9 135.3 %copy-start = (f32[4608]{0:T(1024)S(1)}, f32[4608]{0:T(1024)}, u32[]{:S(2)}) copy-start(f32[4608]{0:T(1024)} %param.13) | copy-start | bytes 55300
Sparse Core Ops, SparseCore 0:
  8.9 25.4 all-gather.2
  62.1 135.1 all-reduce.2
where the time goes:
time: 229 us
  waiting for transfers between devices  160 us (70%)
  matrix products  27.5 us (12%)
  blocking collectives  21.9 us (10%)
  between operations  13.4 us (6%)
  other arithmetic  5.42 us (2%)
    unnamed x3, waiting for transfers between devices  135 us
    dot_general x1, matrix products, body(): jnp.dot(clamped, dec_weight, preferred_element_type=jnp.float32)  27.5 us
    all_gather x1, waiting for transfers between devices, body(): lax.all_gather(resid, 'dp', axis=0, tiled=True)  24.8 us
    all_gather x1, blocking collectives, body(): steered = lax.all_gather(scaled, 'latent', axis=0, tiled=True)  21.9 us
  transfers between devices with their start and end apart: 2, of which 2 were waited for; matrix products, arithmetic and copies ran while one was open for 1% of the time, Pallas kernels for 0%

commit v1 on v0

v1 whole, which is shorter than its diff:
```python
import functools

import jax
import jax.numpy as jnp
from jax import lax
from jax.experimental import pallas as pl
from jax.experimental.pallas import tpu as pltpu
from jax.sharding import PartitionSpec as P

gate_width = 0.1
norm_eps = 1e-06
no_target = -3.0e38

MESH = pl.DeviceIdType.MESH
WIDTH = 512
HALF = 256
QUART = 128
PIECES = 3
LAGS = (1, 2, 3, 4, 5)


def kernel(
    sizes,
    ids_ref,
    levels_ref,
    resid_ref,
    enc_ref,
    bias_ref,
    thresh_ref,
    dec_ref,
    dbias_ref,
    out_ref,
    wbuf,
    xfull,
    acts,
    targ,
    own,
    pair_tx,
    pair_rx,
    y_own,
    y_tx,
    y_rx,
    x_own,
    x_tx,
    x_rx,
    z_tx,
    z_rx,
    recon,
    w_sem,
    loc_sem,
    g_ssem,
    g_rsem,
    f_ssem,
    f_rsem,
    pair_ssem,
    pair_rsem,
    y_ssem,
    y_rsem,
    x_ssem,
    x_rsem,
    z_ssem,
    z_rsem,
    a_ssem,
    a_rsem,
    b_ssem,
    b_rsem,
):
    n_dp, n_z, n_x, slots = sizes
    rows, width = resid_ref.shape
    lat_dev = enc_ref.shape[1]
    n_enc = lat_dev // WIDTH
    n_dec = width // WIDTH
    z_rows = rows // n_z
    h_rows = rows // 2
    piece = width // PIECES
    dp = lax.axis_index("dp")
    lat = lax.axis_index("latent")
    core = lax.rem(lat, 2)
    chip = lax.div(lat, 2)
    x = lax.rem(chip, n_x)
    z = lax.div(chip, n_x)
    xh = lax.rem(x, 2)
    x_pair = x + 1 - 2 * xh

    def lat_of(z_, x_, core_):
        return (z_ * n_x + x_) * 2 + core_

    partner = (dp, lat_of(z, x, 1 - core))
    dp_peers = [(lax.rem(dp + o, n_dp), lat) for o in range(1, n_dp)]
    x_index = [lax.rem(x + o, n_x) for o in range(1, n_x)]
    x_peers = [(dp, lat_of(z, xo, core)) for xo in x_index]
    z_index = [lax.rem(z + o, n_z) for o in range(1, n_z)]
    z_peers = [(dp, lat_of(zo, x, core)) for zo in z_index]
    fwd_peers = [
        partner,
        (dp, lat_of(z, x_pair, core)),
        (dp, lat_of(z, x_pair, 1 - core)),
    ]

    def enc_copy(i):
        cols = pl.ds(pl.multiple_of(i * WIDTH, WIDTH), WIDTH)
        return pltpu.make_async_copy(enc_ref.at[:, cols], wbuf.at[i], w_sem.at[i])

    def dec_slot(j):
        return lax.rem(j + slots - (slots - n_enc), slots) if slots > n_enc else lax.rem(j, slots)

    def dec_copy(j):
        cols = pl.ds(pl.multiple_of(j * WIDTH, WIDTH), WIDTH)
        s = dec_slot(j)
        return pltpu.make_async_copy(
            dec_ref.at[:, cols], wbuf.at[s, pl.ds(0, lat_dev)], w_sem.at[s]
        )

    def remote(src, dst, ssem, rsem, device):
        return pltpu.make_async_remote_copy(
            src_ref=src, dst_ref=dst, send_sem=ssem, recv_sem=rsem,
            device_id=device, device_id_type=MESH,
        )

    def start_enc(i, _):
        enc_copy(i).start()
        return 0

    lax.fori_loop(0, n_enc, start_enc, 0)
    ahead = slots - n_enc
    for j in range(ahead):
        dec_copy(j).start()
    own_rows = pl.ds(pl.multiple_of(dp * rows, rows), rows)
    local = pltpu.make_async_copy(resid_ref, xfull.at[own_rows], loc_sem)
    local.start()

    barrier = pltpu.get_barrier_semaphore()
    greeted = dp_peers + x_peers + z_peers + [fwd_peers[0], fwd_peers[2]]
    for device in greeted:
        pl.semaphore_signal(barrier, inc=1, device_id=device, device_id_type=MESH)
    pl.semaphore_wait(barrier, len(greeted))

    def gather(o, s):
        cols = pl.ds(s * piece, piece)
        src_rows = pl.ds(pl.multiple_of(core * h_rows, 16), h_rows)
        dst_rows = pl.ds(pl.multiple_of(dp * rows + core * h_rows, 16), h_rows)
        return remote(
            resid_ref.at[src_rows, cols], xfull.at[dst_rows, cols],
            g_ssem.at[o, s], g_rsem.at[o, s], dp_peers[o],
        )

    def forward(o, s):
        cols = pl.ds(s * piece, piece)
        origin = lax.rem(dp + n_dp - (o + 1), n_dp)
        r = pl.ds(pl.multiple_of(origin * rows + core * h_rows, 16), h_rows)
        return remote(
            xfull.at[r, cols], xfull.at[r, cols], f_ssem.at[o, s], f_rsem.at[o, s], partner
        )

    pairs = [(o, s) for s in range(PIECES) for o in range(n_dp - 1)]
    for o, s in pairs:
        gather(o, s).start()

    first_col = (dp * lax.axis_size("latent") + lat) * lat_dev
    columns = first_col + lax.broadcasted_iota(jnp.int32, (1, lat_dev), 1)
    thresh_all = thresh_ref[...]
    targets = jnp.full((1, lat_dev), no_target, jnp.float32)
    for k in range(ids_ref.shape[0]):
        level = levels_ref[k].astype(jnp.float32)
        targets = jnp.where(
            columns == ids_ref[k], jnp.maximum(targets, level * thresh_all), targets
        )
    targ[...] = targets

    for o, s in pairs:
        gather(o, s).wait_recv()
        forward(o, s).start()
    local.wait()
    for o, s in pairs:
        forward(o, s).wait_recv()

    def encode(i, _):
        cols = pl.ds(pl.multiple_of(i * WIDTH, WIDTH), WIDTH)
        enc_copy(i).wait()
        pre = jnp.dot(xfull[...], wbuf[i], preferred_element_type=jnp.float32) + bias_ref[:, cols]
        act = pre * jax.nn.sigmoid((pre - thresh_ref[:, cols]) / gate_width)
        acts[:, cols] = jnp.maximum(act, targ[:, cols]).astype(jnp.bfloat16)

        @pl.when(i + ahead < n_dec)
        def _():
            dec_copy(i + ahead).start()

        return 0

    lax.fori_loop(0, n_enc, encode, 0)

    def pair_copy(k):
        return remote(pair_tx.at[k], pair_rx.at[k], pair_ssem.at[k], pair_rsem.at[k], partner)

    def y_copy(k, o):
        return remote(
            y_tx.at[k, o], y_rx.at[k, o], y_ssem.at[k, o], y_rsem.at[k, o], dp_peers[o]
        )

    def x_copy(k, o):
        return remote(x_tx.at[k, o], x_rx.at[k, o], x_ssem.at[k, o], x_rsem.at[k, o], x_peers[o])

    def z_copy(k, o):
        return remote(z_tx.at[k, o], z_rx.at[k, o], z_ssem.at[k, o], z_rsem.at[k, o], z_peers[o])

    def own_cols(k):
        return pl.ds(pl.multiple_of(k * WIDTH + core * HALF + xh * QUART, QUART), QUART)

    def a_copy(k, o):
        ref = recon.at[pl.ds(pl.multiple_of(z * z_rows, 16), z_rows), own_cols(k)]
        return remote(ref, ref, a_ssem.at[k, o], a_rsem.at[k, o], z_peers[o])

    def b_copy(k, o):
        ref = recon.at[:, own_cols(k)]
        return remote(ref, ref, b_ssem.at[k, o], b_rsem.at[k, o], fwd_peers[o])

    def decode(k):
        dec_copy(k).wait()
        part = jnp.dot(
            acts[...], wbuf[dec_slot(k), :lat_dev], preferred_element_type=jnp.float32
        )
        low, high = part[:, :HALF], part[:, HALF:]
        own[lax.rem(k, 2)] = jnp.where(core == 0, low, high)
        pair_tx[k] = jnp.where(core == 0, high, low).astype(jnp.bfloat16)
        pair_copy(k).start()

        if n_enc + ahead < n_dec:

            @pl.when(k + n_enc + ahead < n_dec)
            def _():
                dec_copy(k + n_enc + ahead).start()

    def after_pair(k):
        pair_copy(k).wait_recv()
        slot = lax.rem(k, 2)

        def rows_of(q):
            r = pl.ds(pl.multiple_of(q * rows, rows), rows)
            return own[slot, r] + pair_rx[k, r].astype(jnp.float32)

        for o in range(n_dp - 1):
            y_tx[k, o] = rows_of(dp_peers[o][0]).astype(jnp.bfloat16)
            y_copy(k, o).start()
        y_own[k] = rows_of(dp)

    def after_y(k):
        total = y_own[k]
        for o in range(n_dp - 1):
            y_copy(k, o).wait_recv()
            total = total + y_rx[k, o].astype(jnp.float32)
        halves = (total[:, :QUART], total[:, QUART:])
        for o in range(n_x - 1):
            there = jnp.where(lax.rem(x_index[o], 2) == 0, halves[0], halves[1])
            x_tx[k, o] = there.astype(jnp.bfloat16)
            x_copy(k, o).start()
        x_own[k] = jnp.where(xh == 0, halves[0], halves[1])

    def after_x(k):
        total = x_own[k]
        for o in range(n_x - 1):
            x_copy(k, o).wait_recv()
            total = total + x_rx[k, o].astype(jnp.float32)
        x_own[k] = total
        for o in range(n_z - 1):
            r = pl.ds(pl.multiple_of(z_index[o] * z_rows, z_rows), z_rows)
            z_tx[k, o] = x_own[k, r].astype(jnp.bfloat16)
            z_copy(k, o).start()

    def after_z(k):
        total = x_own[k, pl.ds(pl.multiple_of(z * z_rows, z_rows), z_rows)]
        for o in range(n_z - 1):
            z_copy(k, o).wait_recv()
            total = total + z_rx[k, o].astype(jnp.float32)
        total = total + dbias_ref[:, own_cols(k)]
        r = pl.ds(pl.multiple_of(z * z_rows, 16), z_rows)
        recon[r, own_cols(k)] = total.astype(jnp.bfloat16)
        for o in range(n_z - 1):
            a_copy(k, o).start()

    def after_gather(k):
        for o in range(n_z - 1):
            a_copy(k, o).wait_recv()
        for o in range(3):
            b_copy(k, o).start()

    stages = (after_pair, after_y, after_x, after_z, after_gather)

    def step(it, _):
        @pl.when(it < n_dec)
        def _():
            decode(it)

        for stage, lag in zip(stages, LAGS):

            @pl.when(jnp.logical_and(it >= lag, it < n_dec + lag))
            def _(stage=stage, lag=lag):
                stage(it - lag)

        return 0

    lax.fori_loop(0, n_dec + LAGS[-1], step, 0)

    resid32 = xfull[own_rows].astype(jnp.float32)
    in_sq = jnp.sum(jnp.square(resid32), axis=1, keepdims=True)

    def finish(k, _):
        for o in range(3):
            b_copy(k, o).wait_recv()
        return 0

    lax.fori_loop(0, n_dec, finish, 0)

    full = recon[...].astype(jnp.float32)
    out_sq = jnp.sum(jnp.square(full), axis=1, keepdims=True)
    scale = jnp.sqrt((in_sq + norm_eps) / (out_sq + norm_eps))
    out_ref[...] = (recon[...].astype(jnp.float32) * scale).astype(jnp.bfloat16)

    for o, s in pairs:
        gather(o, s).wait_send()
        forward(o, s).wait_send()

    def sent(k, _):
        pair_copy(k).wait_send()
        for o in range(n_dp - 1):
            y_copy(k, o).wait_send()
        for o in range(n_x - 1):
            x_copy(k, o).wait_send()
        for o in range(n_z - 1):
            z_copy(k, o).wait_send()
            a_copy(k, o).wait_send()
        for o in range(3):
            b_copy(k, o).wait_send()
        return 0

    lax.fori_loop(0, n_dec, sent, 0)


def body(n_dp, n_lat, resid, enc_weight, enc_bias, thresholds, dec_weight, dec_bias, ids, levels):
    rows, width = resid.shape
    lat_dev = enc_weight.shape[1]
    tokens = rows * n_dp
    n_enc, n_dec = lat_dev // WIDTH, width // WIDTH
    n_z = 4
    n_x = n_lat // (2 * n_z)
    slots = n_enc + 1 if tokens <= 256 else n_enc
    z_rows = rows // n_z
    bf16, f32 = jnp.bfloat16, jnp.float32
    dma = pltpu.SemaphoreType.DMA
    anywhere = pl.BlockSpec(memory_space=pl.ANY)
    vmem = pl.BlockSpec(memory_space=pltpu.VMEM)
    smem = pl.BlockSpec(memory_space=pltpu.SMEM)
    return pl.pallas_call(
        functools.partial(kernel, (n_dp, n_z, n_x, slots)),
        out_shape=jax.ShapeDtypeStruct((rows, width), bf16),
        in_specs=[smem, smem, anywhere, anywhere, vmem, vmem, anywhere, vmem],
        out_specs=vmem,
        scratch_shapes=[
            pltpu.VMEM((slots, width, WIDTH), bf16),
            pltpu.VMEM((tokens, width), bf16),
            pltpu.VMEM((tokens, lat_dev), bf16),
            pltpu.VMEM((1, lat_dev), f32),
            pltpu.VMEM((2, tokens, HALF), f32),
            pltpu.VMEM((n_dec, tokens, HALF), bf16),
            pltpu.VMEM((n_dec, tokens, HALF), bf16),
            pltpu.VMEM((n_dec, rows, HALF), f32),
            pltpu.VMEM((n_dec, n_dp - 1, rows, HALF), bf16),
            pltpu.VMEM((n_dec, n_dp - 1, rows, HALF), bf16),
            pltpu.VMEM((n_dec, rows, QUART), f32),
            pltpu.VMEM((n_dec, n_x - 1, rows, QUART), bf16),
            pltpu.VMEM((n_dec, n_x - 1, rows, QUART), bf16),
            pltpu.VMEM((n_dec, n_z - 1, z_rows, QUART), bf16),
            pltpu.VMEM((n_dec, n_z - 1, z_rows, QUART), bf16),
            pltpu.VMEM((rows, width), bf16),
            dma((slots,)),
            dma,
            dma((n_dp - 1, PIECES)),
            dma((n_dp - 1, PIECES)),
            dma((n_dp - 1, PIECES)),
            dma((n_dp - 1, PIECES)),
            dma((n_dec,)),
            dma((n_dec,)),
            dma((n_dec, n_dp - 1)),
            dma((n_dec, n_dp - 1)),
            dma((n_dec, n_x - 1)),
            dma((n_dec, n_x - 1)),
            dma((n_dec, n_z - 1)),
            dma((n_dec, n_z - 1)),
            dma((n_dec, n_z - 1)),
            dma((n_dec, n_z - 1)),
            dma((n_dec, 3)),
            dma((n_dec, 3)),
        ],
        compiler_params=pltpu.CompilerParams(
            collective_id=0, has_side_effects=True, vmem_limit_bytes=60 * 2**20
        ),
    )(
        ids,
        levels,
        resid,
        enc_weight,
        enc_bias.reshape(1, lat_dev),
        thresholds.reshape(1, lat_dev),
        dec_weight,
        dec_bias.reshape(1, width),
    )


def solution(mesh):
    in_specs = (
        P("dp", None),
        P(None, ("dp", "latent")),
        P(("dp", "latent")),
        P(("dp", "latent")),
        P(("dp", "latent"), None),
        P(),
        P(),
        P(),
    )
    return jax.shard_map(
        functools.partial(body, mesh.shape["dp"], mesh.shape["latent"]),
        mesh=mesh,
        in_specs=in_specs,
        out_specs=P("dp", None),
        check_vma=False,
    )
```

time: 229 us -> 69.2 us (0.30)
  waiting for transfers between devices: 160 us -> 0 us
  Pallas kernels: 0 us -> 65.7 us
  matrix products: 27.5 us -> 0 us
  blocking collectives: 21.9 us -> 0 us
  between operations: 13.4 us -> 0.01 us
  other arithmetic: 5.42 us -> 0 us
  local copies, waits for them, and re-layouts: 0.95 us -> 3.26 us
    unnamed x3 -> x0, waiting for transfers between devices: 135 us -> none
    pallas_call x0 -> x1, Pallas kernels: none -> 65.7 us  [body(): pl.pallas_call(functools.partial(kernel, (n_dp, n_z, n_x, slots)), out_sh...]
    dot_general x1 -> x0, matrix products: 27.5 us -> none  [body(): jnp.dot(clamped, dec_weight, preferred_element_type=jnp.float32)]
    all_gather x1 -> x0, waiting for transfers between devices: 24.8 us -> none  [body(): lax.all_gather(resid, 'dp', axis=0, tiled=True)]
    all_gather x1 -> x0, blocking collectives: 21.9 us -> none  [body(): steered = lax.all_gather(scaled, 'latent', axis=0, tiled=True)]
  transfers between devices with their start and end apart: 2 -> 0, of which waited for: 2 -> 0; matrix products, arithmetic and copies ran while one was open for 1% -> 0% of each run, Pallas kernels for 0% -> 0%
where the time goes in v1:
time: 69.2 us; the launch traced here: 68.9 us
  Pallas kernels  65.7 us (95%)
  local copies, waits for them, and re-layouts  3.26 us (5%)
    pallas_call x1, Pallas kernels, body(): pl.pallas_call(functools.partial(kernel, (n_dp, n_z, n_x, slots)), out_sh...  65.7 us
    unnamed x1, local copies, waits for them, and re-layouts  1.92 us

profile of v1, /device:TPU:0, one launch (start us, length us, event | category | flops | bytes accessed | tf_op | source)
XLA Modules:
  0.0 68.9 jit_solution(2290866239883199608)
XLA Ops:
  0.0 1.3 %reshape.11.dbias_ref = f32[1,4608]{1,0:T(1,128)} reshape(f32[4608]{0:T(1024)} %param.13) | data formatting | bytes 36864 | tf_op jit(solution)/shard_map/reshape | solution.py:404
  1.3 65.7 %shard_map.82 = bf16[64,4608]{1,0:T(8,128)(2,1)} custom-call(s32[16]{0:T(128)} %ids_ref.1, s32[16]{0:T(128)} %levels_ref.1, bf16[64,4608]{1,0:T(8,128)(2,1)} %resid_ref.1, bf16[4608,4096]{1,0:T(8,128)(2,1)} %enc_ref.1, f32[1,4096]{1,0:T(1,128)} %bitcast.2, f32[1,4096]{1,0:T(1,128)} %bitcast.3, bf16[4096,4608]{1,0:T(8,128)(2,1)} %dec_ref.1, ...), custom_call_target="tpu_custom_call" | custom-call | tf_op jit(solution)/shard_map/pallas_call | solution.py:352
  67.0 1.9 %copy.10 = bf16[64,4608]{1,0:T(8,128)(2,1)} copy(bf16[64,4608]{1,0:T(8,128)(2,1)} %shard_map.82) | data formatting | bytes 1179648

commit v2 on v1

--- a/solution.py
+++ b/solution.py
@@ -16,7 +16,7 @@
 HALF = 256
 QUART = 128
 PIECES = 3
-LAGS = (1, 2, 3, 4, 5)
+LAGS = (1, 4, 7, 10, 13)
 
 
 def kernel(
@@ -220,7 +220,7 @@
             acts[...], wbuf[dec_slot(k), :lat_dev], preferred_element_type=jnp.float32
         )
         low, high = part[:, :HALF], part[:, HALF:]
-        own[lax.rem(k, 2)] = jnp.where(core == 0, low, high)
+        own[lax.rem(k, LAGS[0] + 1)] = jnp.where(core == 0, low, high)
         pair_tx[k] = jnp.where(core == 0, high, low).astype(jnp.bfloat16)
         pair_copy(k).start()
 
@@ -232,7 +232,7 @@
 
     def after_pair(k):
         pair_copy(k).wait_recv()
-        slot = lax.rem(k, 2)
+        slot = lax.rem(k, LAGS[0] + 1)
 
         def rows_of(q):
             r = pl.ds(pl.multiple_of(q * rows, rows), rows)
@@ -271,7 +271,8 @@
         for o in range(n_z - 1):
             z_copy(k, o).wait_recv()
             total = total + z_rx[k, o].astype(jnp.float32)
-        total = total + dbias_ref[:, own_cols(k)]
+        bias_row = k * (WIDTH // QUART) + core * (HALF // QUART) + xh
+        total = total + dbias_ref[pl.ds(bias_row, 1), :]
         r = pl.ds(pl.multiple_of(z * z_rows, 16), z_rows)
         recon[r, own_cols(k)] = total.astype(jnp.bfloat16)
         for o in range(n_z - 1):
@@ -359,7 +360,7 @@
             pltpu.VMEM((tokens, width), bf16),
             pltpu.VMEM((tokens, lat_dev), bf16),
             pltpu.VMEM((1, lat_dev), f32),
-            pltpu.VMEM((2, tokens, HALF), f32),
+            pltpu.VMEM((LAGS[0] + 1, tokens, HALF), f32),
             pltpu.VMEM((n_dec, tokens, HALF), bf16),
             pltpu.VMEM((n_dec, tokens, HALF), bf16),
             pltpu.VMEM((n_dec, rows, HALF), f32),
@@ -401,7 +402,7 @@
         enc_bias.reshape(1, lat_dev),
         thresholds.reshape(1, lat_dev),
         dec_weight,
-        dec_bias.reshape(1, width),
+        dec_bias.reshape(width // QUART, QUART),
     )
 
 

time: 69.2 us -> 55.1 us (0.80)
  Pallas kernels: 65.7 us -> 53 us
  local copies, waits for them, and re-layouts: 3.26 us -> 1.92 us
    pallas_call x1, Pallas kernels: 65.7 us -> 53 us  [body(): pl.pallas_call(functools.partial(kernel, (n_dp, n_z, n_x, slots)), out_sh...]
    reshape x1 -> x0, local copies, waits for them, and re-layouts: 1.35 us -> none  [body(): dec_bias.reshape(1, width)]
where the time goes in v2:
time: 55.1 us; the launch traced here: 54.9 us
  Pallas kernels  53 us (96%)
  local copies, waits for them, and re-layouts  1.92 us (3%)
    pallas_call x1, Pallas kernels, body(): pl.pallas_call(functools.partial(kernel, (n_dp, n_z, n_x, slots)), out_sh...  53 us
    unnamed x1, local copies, waits for them, and re-layouts  1.92 us

profile of v2, /device:TPU:0, one launch (start us, length us, event | category | flops | bytes accessed | tf_op | source)
XLA Modules:
  0.0 54.9 jit_solution(13156881117656381277)
XLA Ops:
  0.0 53.0 %shard_map.82 = bf16[64,4608]{1,0:T(8,128)(2,1)} custom-call(s32[16]{0:T(128)} %ids_ref.1, s32[16]{0:T(128)} %levels_ref.1, bf16[64,4608]{1,0:T(8,128)(2,1)} %resid_ref.1, bf16[4608,4096]{1,0:T(8,128)(2,1)} %enc_ref.1, f32[1,4096]{1,0:T(1,128)} %bitcast.4, f32[1,4096]{1,0:T(1,128)} %bitcast.5, bf16[4096,4608]{1,0:T(8,128)(2,1)} %dec_ref.1, f32[36,128]{1,0:T(8,128)} %bitcast.3), custom_call_target="tpu_custom_call" | custom-call | tf_op jit(solution)/shard_map/pallas_call | solution.py:353
  53.0 1.9 %copy.10 = bf16[64,4608]{1,0:T(8,128)(2,1)} copy(bf16[64,4608]{1,0:T(8,128)(2,1)} %shard_map.82) | data formatting | bytes 1179648
